TPU v7x, 128 devices: a whole 4x4x4 slice. The times are simulated.
128 devices in a mesh: row: 8 (over x, y_lo), col: 4 (over z), comp: 4 (over y_hi, core).
Axes of the slice: x: 4, y: 4 (y_hi: 2, y_lo: 2; y = y_hi * 2 + y_lo), z: 4, core: 2. Of those that a mesh axis runs over, the one named last changes fastest.
Arguments:
- features: bfloat16 [256, 1024, 512], P('row', ('col', 'comp')), may hold values from -6 to 6
- conv_weight: bfloat16 [3, 3, 512, 256], replicated, may hold values from -0.09375 to 0.09375
- conv_bias: float32 [256], replicated, may hold values from -3 to 3
- means: float32 [1024, 256], P('comp'), may hold values from -0.6 to 0.6
- precisions: float32 [1024, 256], P('comp'), may hold values from 0.7 to 1.3
- mix_logits: float32 [1024], replicated, may hold values from -4 to 4
- tissue_counts: int32 [8, 16], P('row', ('col', 'comp')), may hold values from 1 to 2048, as said below
Outputs:
- mean_fisher: float32 [1024, 256], P('comp')
- var_fisher: float32 [1024, 256], P('comp')
Inputs may be any that keep to these rules, and one draw needn't show every extreme that they name: `tissue_counts`: a tile of tile row r holds at most 2048 * (r + 1) // 8 tissue patches; some tile is full.
All inputs are finite; a program needn't handle non-finite values.
Results may differ from a plain program's by a relative error of at most 0.0065.
The roundings to bfloat16 on the way count: a program that leaves them out, or rounds other values in their place, can miss the bound.
Values may be sent and summed in bfloat16 or wider, within the bound.
A program may use at most 64 MiB of HBM per device.

v0:
```python
import jax
import jax.numpy as jnp
from jax import lax
from jax.sharding import PartitionSpec as P


def padded_2(cells, sides, width):
    for axis, dim in sides:
        count = lax.axis_size(axis)
        ends = count - 1
        head = lax.slice_in_dim(cells, 0, width, axis=dim)
        tail = lax.slice_in_dim(cells, cells.shape[dim] - width, cells.shape[dim], axis=dim)
        cells = jnp.concatenate(
            [
                lax.ppermute(tail, axis, [(i, (i + 1) % count) for i in range(ends)]),
                cells,
                lax.ppermute(head, axis, [((i + 1) % count, i) for i in range(ends)]),
            ],
            axis=dim,
        )
    return cells


def joined(x, axis, combine):
    everything = jax.tree.map(lambda part: lax.all_gather(part, axis), x)
    leading = jax.tree.map(lambda part: part[0], everything)

    def step(k, so_far):
        return combine(so_far, jax.tree.map(lambda part: part[k], everything))

    return lax.fori_loop(1, lax.axis_size(axis), step, leading)


def conv_block(padded, conv_weight, conv_bias, height, width):
    total_sum = jnp.zeros((height * width, conv_weight.shape[3]), jnp.float32)
    for offset_row in range(3):
        for offset_col in range(3):
            window = padded[
                offset_row : offset_row + height, offset_col : offset_col + width, :
            ].reshape(height * width, padded.shape[2])
            total_sum = total_sum + jnp.dot(
                window, conv_weight[offset_row, offset_col], preferred_element_type=jnp.float32
            )
    encoded = (total_sum + conv_bias).astype(jnp.bfloat16)
    widened = encoded.astype(jnp.float32)
    squared = (widened * widened).astype(jnp.bfloat16)
    return jnp.concatenate([encoded, squared], axis=1)


def build_panel(centres, precisions, log_weights):
    panel = jnp.concatenate(
        [(centres * precisions).astype(jnp.bfloat16), (-0.5 * precisions).astype(jnp.bfloat16)],
        axis=1,
    )
    offset = (
        log_weights
        + 0.5 * jnp.sum(jnp.log(precisions), axis=1)
        - 0.5 * jnp.sum(precisions * centres * centres, axis=1)
    )
    return (panel, offset)


def score_rows(design, panel, offset):
    return (
        lax.dot_general(design, panel, (((1,), (1,)), ((), ())), preferred_element_type=jnp.float32)
        + offset
    )


def moments(gamma, design):
    stats = lax.dot_general(
        gamma, design, (((0,), (0,)), ((), ())), preferred_element_type=jnp.float32
    )
    return (stats, jnp.sum(gamma.astype(jnp.float32), axis=0))


def combine_mass(earlier, later):
    peak = jnp.maximum(earlier[0], later[0])
    mass = earlier[1] * jnp.exp(earlier[0] - peak) + later[1] * jnp.exp(later[0] - peak)
    return (peak, mass)


def finish(stats, zeroth, centres, precisions, log_weights, total):
    width = centres.shape[1]
    first = stats[:, :width]
    second = stats[:, width:]
    weights = jnp.exp(log_weights)
    mean_fisher = (
        (first - centres * zeroth[:, None])
        * jnp.sqrt(precisions)
        / jnp.sqrt(total * weights)[:, None]
    )
    var_fisher = (
        second * precisions
        - 2.0 * centres * precisions * first
        + (centres * centres * precisions - 1.0) * zeroth[:, None]
    ) / jnp.sqrt(2.0 * total * weights)[:, None]
    return (mean_fisher, var_fisher)


def shards(features, conv_weight, conv_bias, means, precisions, mix_logits, tissue_counts):
    height = features.shape[0]
    width = features.shape[1]
    padded = padded_2(features, (("row", 0), (("col", "comp"), 1)), 1)
    design = conv_block(padded, conv_weight, conv_bias, height, width)
    patches = height * width
    limit = tissue_counts[0, 0]
    valid = (jnp.arange(patches, dtype=jnp.int32) < limit).astype(jnp.float32)
    log_weights = jax.nn.log_softmax(mix_logits)
    quarter = means.shape[0]
    first_comp = lax.axis_index("comp") * quarter
    own_logs = lax.dynamic_slice_in_dim(log_weights, first_comp, quarter)
    design_all, valid_all = (
        lax.all_gather(design, "comp", axis=0, tiled=True),
        lax.all_gather(valid.astype(jnp.bfloat16), "comp", axis=0, tiled=True),
    )
    panel, offset = build_panel(means, precisions, own_logs)
    scores = score_rows(design_all, panel, offset)
    peak = jnp.max(scores, axis=1)
    mass = jnp.sum(jnp.exp(scores - peak[:, None]), axis=1)
    peak_all, mass_all = joined((peak, mass), "comp", combine_mass)
    normal = peak_all + jnp.log(mass_all)
    gamma = (jnp.exp(scores - normal[:, None]) * valid_all.astype(jnp.float32)[:, None]).astype(
        jnp.bfloat16
    )
    stats, zeroth = moments(gamma, design_all)
    stats, zeroth = lax.psum((stats, zeroth), ("row", "col"))
    total = lax.psum(limit.astype(jnp.float32), ("row", "col", "comp"))
    return finish(stats, zeroth, means, precisions, own_logs, total)


def solution(mesh):
    in_specs = (
        P("row", ("col", "comp"), None),
        P(),
        P(),
        P("comp", None),
        P("comp", None),
        P(),
        P("row", ("col", "comp")),
    )
    out_specs = (P("comp", None), P("comp", None))
    return jax.shard_map(shards, mesh=mesh, in_specs=in_specs, out_specs=out_specs, check_vma=False)
```

profile of v0, /device:TPU:0, one launch (start us, length us, event | category | flops | bytes accessed | tf_op | source)
XLA Modules:
  0.0 504.7 jit_solution(14844967867681278499)
XLA Ops:
  8.1 3.6 collective-permute-start
  11.7 1.3 collective-permute-start.1
  13.0 2.5 fusion.26
  15.5 2.3 collective-permute-done.1
  18.7 1.3 collective-permute-start.2
  20.0 1.3 collective-permute-start.3
  22.8 3.4 collective-permute-done.3
  26.3 6.3 %fusion.8 = (bf16[32,64,512]{2,1,0:T(8,128)(2,1)S(1)}, bf16[32,64,512]{2,1,0:T(8,128)(2,1)S(1)}, bf16[32,64,512]{2,1,0:T(8,128)(2,1)S(1)}, bf16[32,64,512]{2,1,0...) fusion(bf16[34,64,512]{2,1,0:T(8,128)(2,1)S(1)} %constant_dynamic-update-slice_fusion, ...), kind=kLoop, calls=%fused_computation.25 | loop fusion | flops 25165824 | bytes 14880768 | tf_op jit(solution)/shard_map/concatenate | solution.py:13
  35.7 1.1 fusion.5
  36.8 1.2 multiply_convert_fusion.1
  38.1 1.6 pad_maximum_fusion.4
  40.5 105.8 %psum.23 = f32[]{:T(128)} all-reduce(f32[]{:T(128)S(6)} %convert_element_type.43), channel_id=1, replica_groups=mesh['row'=8,'col'=4,'comp'=4] {'row','col','comp'}, use_global_device_ids=true, to_apply=%region_11.12 | all-reduce | flops 1 | bytes 8 | tf_op jit(solution)/shard_map/psum | solution.py:128
  146.9 1.2 exponential_reduce_fusion.1
  148.8 6.9 %all_gather.23 = bf16[8192]{0:T(1024)(128)(2,1)S(1)} all-gather(bf16[2048]{0:T(1024)(128)(2,1)S(1)} %convert_convert_fusion), channel_id=1, replica_groups=mesh['row'=8,'col'=4,'comp'=4] {'comp'}, dimensions={0}, use_global_device_ids=true | all-gather | bytes 20480 | tf_op jit(solution)/shard_map/all_gather | solution.py:115
  157.9 5.8 %fusion.47 = (f32[8192]{0:T(1024)S(1)}, f32[8192,256]{0,1:T(8,128)S(1)}) fusion(f32[256]{0:T(256)S(1)} %get-tuple-element.175, bf16[8192,512]{0,1:T(8,128)(2,1)} %all-gather.4.cloned.1.call-done, bf16[256,256]{1,0:T(8,128)(2,1)S(1)} %get-tuple-element.172, bf16[256,256]{1,0:T(8,128)(2,1)S(1)} %get-tuple-element.171), kind=kOutput, calls=%fused_computation.87 | convolution fusion | flops 2152194048 | bytes 17073152 | tf_op jit(solution)/shard_map/dot_general | solution.py:65
  163.7 1.2 exponential_reduce_fusion
  164.9 2.0 copy-done
  166.9 6.9 %all-gather.1 = f32[32768]{0:T(1024)S(1)} all-gather(f32[8192]{0:T(1024)S(1)} %exponential_reduce_fusion), channel_id=3, replica_groups=mesh['row'=8,'col'=4,'comp'=4] {'comp'}, dimensions={0}, use_global_device_ids=true | all-gather | bytes 163840 | tf_op jit(solution)/shard_map/all_gather | solution.py:25
  173.9 6.9 %all-gather = f32[32768]{0:T(1024)S(1)} all-gather(f32[8192]{0:T(1024)S(1)} %get-tuple-element.178), channel_id=2, replica_groups=mesh['row'=8,'col'=4,'comp'=4] {'comp'}, dimensions={0}, use_global_device_ids=true | all-gather | bytes 163840 | tf_op jit(solution)/shard_map/all_gather | solution.py:25
  181.3 8.9 %fusion.12 = f32[256,512]{1,0:T(8,128)} fusion(bf16[8192,512]{0,1:T(8,128)(2,1)} %all-gather.4.cloned.1.call-done, f32[8192,256]{0,1:T(8,128)} %copy-done, f32[8192]{0:T(1024)S(1)} %convert_element_type.40, f32[8192]{0:T(1024)S(1)} %log_add_fusion), kind=kOutput, calls=%fused_computation.35 | convolution fusion | flops 2153775104 | bytes 17367040 | tf_op jit(solution)/shard_map/dot_general | solution.py:71
  190.3 4.9 convert_reduce_fusion
  195.2 80.7 %psum.22 = f32[256]{0:T(256)S(1)} all-reduce(f32[256]{0:T(256)S(1)} %convert_reduce_fusion), channel_id=1, replica_groups=mesh['row'=8,'col'=4,'comp'=4] {'row','col'}, use_global_device_ids=true, to_apply=%region_10.11 | all-reduce | flops 256 | bytes 2048 | tf_op jit(solution)/shard_map/psum | solution.py:127
  275.8 220.0 %all-reduce.2.cloned.1.call-done = f32[256,512]{1,0:T(8,128)} async-done(((f32[256,512]{1,0:T(8,128)}), f32[256,512]{1,0:T(8,128)}) %all-reduce.2.cloned.1.call-update) | async-done | bytes 524304 | tf_op jit(solution)/shard_map/psum | solution.py:127
  495.8 2.0 fusion.15
  (49 shorter events, 9.5 us)
Async XLA Ops:
  7.2 150.7 %all-gather.4.cloned.1.call-start = ((), (), s32[]{:S(2)}) async-start(), calls=%async_computation | async-start | bytes 10485760 | tf_op jit(solution)/shard_map/all_gather | solution.py:114
  8.1 7.4 %collective-permute-start = (bf16[1,64,512]{2,1,0:T(8,128)(2,1)S(1)}, bf16[1,64,512]{2,1,0:T(8,128)(2,1)S(1)}, u32[]{:S(2)}, u32[]{:S(2)}) collective-permute-start(bf16[1,64,512]{2,1,0:T(8,128)(2,1)S(1)} %get-tuple-element.168), channel_id=1, source_target_pairs={{0,16},{16,32},{32,48},{48,64},{64,80},{80,96},{96,112},{1,17},{17... | collective-permute-start | bytes 196616 | tf_op jit(solution)/shard_map/ppermute | solution.py:15
  11.7 6.2 %collective-permute-start.1 = (bf16[1,64,512]{2,1,0:T(8,128)(2,1)S(1)}, bf16[1,64,512]{2,1,0:T(8,128)(2,1)S(1)}, u32[]{:S(2)}, u32[]{:S(2)}) collective-permute-start(bf16[1,64,512]{2,1,0:T(8,128)(2,1)S(1)} %get-tuple-element.167), channel_id=1, source_target_pairs={{16,0},{32,16},{48,32},{64,48},{80,64},{96,80},{112,96},{17,1},{33... | collective-permute-start | bytes 196616 | tf_op jit(solution)/shard_map/ppermute | solution.py:17
  13.0 4.9 copy-start.1
  15.5 5.8 %copy-start.2 = (bf16[3,3,512,256]{3,2,1,0:T(8,128)(2,1)S(1)}, bf16[3,3,512,256]{3,2,1,0:T(8,128)(2,1)}, u32[]{:S(2)}) copy-start(bf16[3,3,512,256]{3,2,1,0:T(8,128)(2,1)} %param.10) | copy-start | bytes 7077892
  18.7 4.1 collective-permute-start.2
  20.0 6.3 %collective-permute-start.3 = (bf16[34,1,512]{2,1,0:T(2,128)(2,1)S(1)}, bf16[34,1,512]{2,1,0:T(2,128)(2,1)S(1)}, u32[]{:S(2)}, u32[]{:S(2)}) collective-permute-start(bf16[34,1,512]{2,1,0:T(2,128)(2,1)S(1)} %get-tuple-element.163), channel_id=1, source_target_pairs={{1,0},{2,1},{3,2},{4,3},{5,4},{6,5},{7,6},{8,7},{9,8},{10,9},{11,1... | collective-permute-start | bytes 104456 | tf_op jit(solution)/shard_map/ppermute | solution.py:17
  35.7 1.1 copy-start.6
  39.7 106.5 %copy-start.5 = (f32[1024]{0:T(1024)S(1)}, f32[1024]{0:T(1024)}, u32[]{:S(2)}) copy-start(f32[1024]{0:T(1024)} %param.14) | copy-start | bytes 12292
  39.7 117.3 %copy-start.3 = (f32[256,256]{1,0:T(8,128)S(1)}, f32[256,256]{1,0:T(8,128)}, u32[]{:S(2)}) copy-start(f32[256,256]{1,0:T(8,128)} %param.13) | copy-start | bytes 786436
  39.7 117.3 %copy-start.4 = (f32[256,256]{1,0:T(8,128)S(1)}, f32[256,256]{1,0:T(8,128)}, u32[]{:S(2)}) copy-start(f32[256,256]{1,0:T(8,128)} %param.12) | copy-start | bytes 786436
  39.7 456.1 %all-reduce.2.cloned.1.call-start = ((), (), s32[]{:S(2)}) async-start(), calls=%async_computation.1 | async-start | bytes 1048576 | tf_op jit(solution)/shard_map/psum | solution.py:127
  163.7 3.2 copy-start
Sparse Core Ops, SparseCore 0:
  39.8 69.8 all-gather.3
  190.4 305.3 all-reduce.1
where the time goes:
time: 505 us
  waiting for transfers between devices  226 us (45%)
  blocking collectives  207 us (41%)
  matrix products  24.1 us (5%)
  other arithmetic  20.4 us (4%)
  between operations  16.3 us (3%)
  starting transfers between devices  7.52 us (1%)
    psum x1, waiting for transfers between devices, shards(): stats, zeroth = lax.psum((stats, zeroth), ('row', 'col'))  220 us
    psum x1, blocking collectives, shards(): total = lax.psum(limit.astype(jnp.float32), ('row', 'col', 'comp'))  106 us
    psum x1, blocking collectives, shards(): stats, zeroth = lax.psum((stats, zeroth), ('row', 'col'))  80.7 us
    all_gather x2, blocking collectives, joined(): everything = jax.tree.map(lambda part: lax.all_gather(part, axis), x)  13.8 us
  transfers between devices with their start and end apart: 6, of which 3 were waited for; matrix products, arithmetic and copies ran while one was open for 2% of the time, Pallas kernels for 0%

commit v1 on v0

v1 whole, which is shorter than its diff:
```python
import functools

import jax
import jax.numpy as jnp
from jax import lax
from jax.experimental import pallas as pl
from jax.experimental.pallas import tpu as pltpu
from jax.sharding import PartitionSpec as P

F32 = jnp.float32
BF16 = jnp.bfloat16
MESH = pl.DeviceIdType.MESH

HEIGHT, WIDTH, CHAN, DIM = 32, 64, 512, 256
COMPS, BLOCK = 1024, 256
PATCHES = HEIGHT * WIDTH
CHUNK = 512
ROWS = CHUNK // WIDTH
CHIPS = 64
GROUP = 32
LANES = 2 * 128 + 128


def signal(sem, device):
    pl.semaphore_signal(sem, inc=1, device_id=device, device_id_type=MESH)


def remote(src, dst, send_sem, recv_sem, device):
    return pltpu.make_async_remote_copy(
        src_ref=src, dst_ref=dst, send_sem=send_sem, recv_sem=recv_sem,
        device_id=device, device_id_type=MESH,
    )


def column(line):
    return jnp.broadcast_to(line, (128, 128)).T


def kernel(
    features, conv_weight, bias, means, precisions, logits, count, out,
    x, w, sides, corners, edge, panel, offset_lines, offsets, own_logs, design, gamma, zeroth,
    give, take, held, landed, gathered,
    load_sem, halo_send, halo_recv, panel_send, panel_recv, pair_send, pair_recv,
    scatter_send, scatter_recv, gather_send, gather_recv,
):
    row, col, comp = lax.axis_index("row"), lax.axis_index("col"), lax.axis_index("comp")
    core = lax.rem(comp, 2)
    upper = comp // 2
    tile = col * 4 + comp
    me = row * 8 + col * 2 + upper
    partner = (row, col, comp + 1 - 2 * core)
    across = (row + 1 - 2 * lax.rem(row, 2), col, lax.rem(comp + 2, 4))

    def chip(number):
        return (number // 8, lax.rem(number // 2, 4), 2 * lax.rem(number, 2) + core)

    def spot(down, right):
        there = tile + right
        return (row + down, there // 4, lax.rem(there, 4))

    def exists(down, right):
        ok = jnp.bool_(True)
        if down < 0:
            ok = row > 0
        if down > 0:
            ok = row < 7
        if right < 0:
            ok = jnp.logical_and(ok, tile > 0)
        if right > 0:
            ok = jnp.logical_and(ok, tile < 15)
        return ok

    load_x = pltpu.make_async_copy(features, x.at[pl.ds(1, HEIGHT)], load_sem.at[0])
    load_w = pltpu.make_async_copy(conv_weight, w, load_sem.at[1])
    load_x.start()
    load_w.start()

    barrier = pltpu.get_barrier_semaphore()

    def greet(step, carry):
        signal(barrier, chip(lax.rem(me + step, CHIPS)))
        return carry

    lax.fori_loop(1, CHIPS, greet, 0)
    signal(barrier, partner)
    diagonal = [(0, -1), (0, 1), (-1, -1), (-1, 1), (1, -1), (1, 1)]
    greeted = CHIPS
    for place in diagonal:
        @pl.when(exists(*place))
        def _():
            signal(barrier, spot(*place))
        greeted = greeted + exists(*place).astype(jnp.int32)

    centres = means[...]
    inverse = precisions[...]
    panel[comp] = jnp.concatenate(
        [(centres * inverse).astype(BF16), (-0.5 * inverse).astype(BF16)], axis=1
    )
    lines = logits[...]
    top = jnp.max(jnp.max(lines, axis=0), axis=1, keepdims=True)
    norm = top + jnp.log(jnp.sum(jnp.sum(jnp.exp(lines - top[None]), axis=0), axis=1, keepdims=True))
    logs = jnp.concatenate([column(logits[2 * comp] - norm), column(logits[2 * comp + 1] - norm)], axis=0)
    own_logs[...] = logs
    constant = 0.5 * jnp.sum(jnp.log(inverse), axis=1, keepdims=True) - 0.5 * jnp.sum(
        inverse * centres * centres, axis=1, keepdims=True
    )
    own_offset = logs + constant
    for half in range(2):
        offset_lines[comp, half] = own_offset[half * 128 : half * 128 + 128].T[:8]

    pl.semaphore_wait(barrier, greeted)

    def panel_copies(block, slot, device):
        return [
            remote(panel.at[block], panel.at[block], panel_send.at[slot, 0], panel_recv.at[slot, 0], device),
            remote(offset_lines.at[block], offset_lines.at[block], panel_send.at[slot, 1], panel_recv.at[slot, 1], device),
        ]

    far = lax.rem(comp + 2, 4)
    to_across = panel_copies(comp, 0, across)
    to_partner = panel_copies(comp, 1, partner)
    onward = panel_copies(far, 2, partner)

    load_x.wait()
    halos = []

    def halo(index, down, right, src, dst):
        halos.append((index, down, right, remote(src, dst, halo_send.at[index], halo_recv.at[index], spot(down, right))))
        @pl.when(exists(down, right))
        def _():
            halos[-1][3].start()

    halo(0, -1, 0, x.at[1], x.at[HEIGHT + 1])
    halo(1, 1, 0, x.at[HEIGHT], x.at[0])
    halo(2, -1, -1, x.at[1, pl.ds(0, 16)], corners.at[1, 1])
    halo(3, -1, 1, x.at[1, pl.ds(WIDTH - 16, 16)], corners.at[0, 1])
    halo(4, 1, -1, x.at[HEIGHT, pl.ds(0, 16)], corners.at[1, 0])
    halo(5, 1, 1, x.at[HEIGHT, pl.ds(WIDTH - 16, 16)], corners.at[0, 0])
    flat = x[1 : HEIGHT + 1].reshape(PATCHES, CHAN)
    line = lax.broadcasted_iota(jnp.int32, (2 * HEIGHT, PATCHES), 0)
    patch = lax.broadcasted_iota(jnp.int32, (2 * HEIGHT, PATCHES), 1)
    wanted = jnp.where(line < HEIGHT, line * WIDTH, (line - HEIGHT) * WIDTH + WIDTH - 1)
    picked = jnp.dot(
        jnp.where(patch == wanted, 1.0, 0.0).astype(BF16), flat, preferred_element_type=F32
    ).astype(BF16)
    edge[0] = picked[:HEIGHT]
    edge[1] = picked[HEIGHT:]
    halo(6, 0, -1, edge.at[0], sides.at[1])
    halo(7, 0, 1, edge.at[1], sides.at[0])
    for copy in to_across + to_partner:
        copy.start()

    @pl.when(row == 0)
    def _():
        x[0] = jnp.zeros((WIDTH, CHAN), BF16)

    @pl.when(row == 7)
    def _():
        x[HEIGHT + 1] = jnp.zeros((WIDTH, CHAN), BF16)

    for side, edge_tile in ((0, 0), (1, 15)):
        @pl.when(tile == edge_tile)
        def _():
            sides[side] = jnp.zeros((HEIGHT, CHAN), BF16)

        for end, edge_row in ((0, 0), (1, 7)):
            @pl.when(jnp.logical_or(tile == edge_tile, row == edge_row))
            def _():
                corners[side, end] = jnp.zeros((16, CHAN), BF16)

    load_w.wait()
    for index, down, right, copy in halos:
        @pl.when(exists(down, right))
        def _():
            copy.wait_send()

        @pl.when(exists(-down, -right))
        def _():
            copy.wait_recv()

    beside = []
    for side, tap, at in ((0, 0, 15), (1, 2, 0)):
        lhs = jnp.concatenate([sides[side], corners[side, 0], corners[side, 1]], axis=0)
        y = [jnp.dot(lhs, w[k, tap], preferred_element_type=F32) for k in range(3)]
        r = lax.broadcasted_iota(jnp.int32, (HEIGHT, DIM), 0)
        above = jnp.where(r == 0, y[0][32 + at : 33 + at], pltpu.roll(y[0][:HEIGHT], 1, 0))
        below = jnp.where(r == HEIGHT - 1, y[2][48 + at : 49 + at], pltpu.roll(y[2][:HEIGHT], HEIGHT - 1, 0))
        beside.append(above + y[1][:HEIGHT] + below)

    c = lax.broadcasted_iota(jnp.int32, (ROWS, WIDTH, DIM), 1)
    for i in range(PATCHES // CHUNK):
        lhs = jnp.concatenate(
            [x[i * ROWS + k : i * ROWS + k + ROWS].reshape(CHUNK, CHAN) for k in range(3)], axis=1
        )
        y = [
            jnp.dot(lhs, w[:, tap].reshape(3 * CHAN, DIM), preferred_element_type=F32)
            for tap in range(3)
        ]
        left, right = (b[i * ROWS : i * ROWS + ROWS].reshape(ROWS, 1, DIM) for b in beside)
        before = jnp.where(c == 0, left, pltpu.roll(y[0], 1, 0).reshape(ROWS, WIDTH, DIM))
        after = jnp.where(c == WIDTH - 1, right, pltpu.roll(y[2], CHUNK - 1, 0).reshape(ROWS, WIDTH, DIM))
        encoded = (y[1].reshape(ROWS, WIDTH, DIM) + before + after + bias[...].reshape(1, 1, DIM)).reshape(CHUNK, DIM).astype(BF16)
        wide = encoded.astype(F32)
        design[i * CHUNK : (i + 1) * CHUNK, :DIM] = encoded
        design[i * CHUNK : (i + 1) * CHUNK, DIM:] = (wide * wide).astype(BF16)

    for copy in to_across + to_partner:
        copy.wait()
    for copy in onward:
        copy.start()
    for copy in onward:
        copy.wait()
    for block in range(4):
        for half in range(2):
            offsets[block, half * 128 : half * 128 + 128] = column(offset_lines[block, half, :1])

    limit = count[...]
    for i in range(PATCHES // CHUNK):
        flipped = design[i * CHUNK : (i + 1) * CHUNK, :DIM].T
        wide = flipped.astype(F32)
        rhs = jnp.concatenate([flipped, (wide * wide).astype(BF16)], axis=0)
        scores = jnp.dot(panel[...].reshape(COMPS, 2 * DIM), rhs, preferred_element_type=F32)
        scores = scores + jnp.concatenate([offsets[...].reshape(COMPS, 128)] * (CHUNK // 128), axis=1)
        peak = jnp.max(scores, axis=0, keepdims=True)
        mass = jnp.exp(scores - peak)
        where = lax.broadcasted_iota(jnp.int32, (1, CHUNK), 1) + i * CHUNK
        scale = jnp.where(where < limit, 1.0 / jnp.sum(mass, axis=0, keepdims=True), 0.0)
        weight = (mass * scale).astype(BF16)
        gamma[:, i * CHUNK : (i + 1) * CHUNK] = weight
        weight = weight.astype(F32)
        part = weight[:, :128]
        for k in range(1, CHUNK // 128):
            part = part + weight[:, k * 128 : k * 128 + 128]
        if i == 0:
            zeroth[...] = part
        else:
            zeroth[...] += part

    tally = jnp.broadcast_to(limit, (8, 128))
    high = tally // 64
    at = lax.broadcasted_iota(jnp.int32, (8, 128), 0)
    counts = jnp.where(at == 0, high, jnp.where(at == 1, tally - high * 64, 0)).astype(F32)

    def statistics(block):
        rows = pl.ds(pl.multiple_of(block * BLOCK, BLOCK), BLOCK)
        stats = jnp.dot(gamma[rows, :], design[...], preferred_element_type=F32)
        main = jnp.concatenate(
            [stats[:, :DIM].reshape(GROUP, 8, DIM), stats[:, DIM:].reshape(GROUP, 8, DIM)], axis=1
        )
        extra = jnp.concatenate(
            [zeroth[rows, :].reshape(GROUP, 8, 128), jnp.broadcast_to(counts[None], (GROUP, 8, 128))], axis=1
        )
        return jnp.concatenate([main, extra], axis=2)

    pair = []
    for k in range(2):
        give[k] = statistics(2 * k + 1 - core).astype(BF16)
        pair.append(remote(give.at[k], take.at[k], pair_send.at[k], pair_recv.at[k], partner))
        pair[k].start()
    for k in range(2):
        mine = statistics(2 * k + core)
        pair[k].wait()
        held[k] = (mine + take[k].astype(F32)).astype(BF16)

    def scatter(step, carry):
        to = lax.rem(me + step, CHIPS)
        device = chip(to)
        remote(
            held.at[lax.rem(to, 2), to // 2], landed.at[CHIPS - step], scatter_send, scatter_recv, device
        ).start()
        return carry

    lax.fori_loop(1, CHIPS, scatter, 0)
    landed[0] = held[upper, row * 4 + col]
    everyone = remote(landed.at[pl.ds(1, CHIPS - 1)], landed.at[pl.ds(1, CHIPS - 1)], scatter_send, scatter_recv, partner)
    everyone.wait_send()
    everyone.wait_recv()
    total = jnp.sum(landed[...].astype(F32), axis=0)
    first = total[:8, :DIM]
    second = total[8:, :DIM]
    mass = jnp.sum(total[:8, DIM:], axis=1, keepdims=True)
    patches = total[8:9, DIM : DIM + 1] * 64.0 + total[9:10, DIM : DIM + 1]
    owner = row * 4 + col
    rows = pl.ds(pl.multiple_of(owner * 8, 8), 8)
    centre = means[rows, :]
    inverse = precisions[rows, :]
    share = jnp.exp(own_logs[rows, :1])
    mean_fisher = (first - centre * mass) * jnp.sqrt(inverse) / jnp.sqrt(patches * share)
    var_fisher = (
        second * inverse - 2.0 * centre * inverse * first + (centre * centre * inverse - 1.0) * mass
    ) / jnp.sqrt(2.0 * patches * share)
    gathered[owner] = jnp.concatenate([mean_fisher, var_fisher], axis=0).astype(BF16)

    def gather(step, carry):
        to = lax.rem(owner + step, GROUP)
        remote(
            gathered.at[owner], gathered.at[owner], gather_send, gather_recv, (to // 4, lax.rem(to, 4), comp)
        ).start()
        return carry

    lax.fori_loop(1, GROUP, gather, 0)
    others = remote(gathered.at[pl.ds(1, GROUP - 1)], gathered.at[pl.ds(1, GROUP - 1)], gather_send, gather_recv, partner)
    others.wait_send()
    others.wait_recv()
    out[...] = gathered[...]


def shards(features, conv_weight, conv_bias, means, precisions, mix_logits, tissue_counts):
    vmem = pl.BlockSpec(memory_space=pltpu.VMEM)
    anywhere = pl.BlockSpec(memory_space=pl.ANY)
    dma = pltpu.SemaphoreType.DMA
    fisher = pl.pallas_call(
        kernel,
        out_shape=jax.ShapeDtypeStruct((GROUP, 16, DIM), BF16),
        in_specs=[anywhere, anywhere, vmem, vmem, vmem, vmem, vmem],
        out_specs=vmem,
        scratch_shapes=[
            pltpu.VMEM((HEIGHT + 2, WIDTH, CHAN), BF16),
            pltpu.VMEM((3, 3, CHAN, DIM), BF16),
            pltpu.VMEM((2, HEIGHT, CHAN), BF16),
            pltpu.VMEM((2, 2, 16, CHAN), BF16),
            pltpu.VMEM((2, HEIGHT, CHAN), BF16),
            pltpu.VMEM((4, BLOCK, 2 * DIM), BF16),
            pltpu.VMEM((4, 2, 8, 128), F32),
            pltpu.VMEM((4, BLOCK, 128), F32),
            pltpu.VMEM((BLOCK, 128), F32),
            pltpu.VMEM((PATCHES, 2 * DIM), BF16),
            pltpu.VMEM((COMPS, PATCHES), BF16),
            pltpu.VMEM((COMPS, 128), F32),
            pltpu.VMEM((2, GROUP, 16, LANES), BF16),
            pltpu.VMEM((2, GROUP, 16, LANES), BF16),
            pltpu.VMEM((2, GROUP, 16, LANES), BF16),
            pltpu.VMEM((CHIPS, 16, LANES), BF16),
            pltpu.VMEM((GROUP, 16, DIM), BF16),
            dma((2,)), dma((8,)), dma((8,)), dma((3, 2)), dma((3, 2)), dma((2,)), dma((2,)),
            dma, dma, dma, dma,
        ],
        compiler_params=pltpu.CompilerParams(
            collective_id=0, has_side_effects=True, vmem_limit_bytes=48 * 2**20
        ),
    )(
        features, conv_weight, conv_bias.reshape(1, DIM), means, precisions,
        mix_logits.reshape(8, 1, 128), tissue_counts,
    )
    fisher = fisher.astype(F32)
    return (fisher[:, :8].reshape(BLOCK, DIM), fisher[:, 8:].reshape(BLOCK, DIM))


def solution(mesh):
    in_specs = (
        P("row", ("col", "comp"), None),
        P(),
        P(),
        P("comp", None),
        P("comp", None),
        P(),
        P("row", ("col", "comp")),
    )
    out_specs = (P("comp", None), P("comp", None))
    return jax.shard_map(shards, mesh=mesh, in_specs=in_specs, out_specs=out_specs, check_vma=False)
```

time: 505 us -> 62.1 us (0.12)
  waiting for transfers between devices: 226 us -> 0 us
  blocking collectives: 207 us -> 0 us
  Pallas kernels: 0 us -> 53.1 us
  matrix products: 24.1 us -> 0 us
  other arithmetic: 20.4 us -> 0.05 us
  between operations: 16.3 us -> 1.31 us
  starting transfers between devices: 7.52 us -> 0 us
    psum x1 -> x0, waiting for transfers between devices: 220 us -> none  [shards(): stats, zeroth = lax.psum((stats, zeroth), ('row', 'col'))]
    psum x2 -> x0, blocking collectives: 186 us -> none  [the longest x1 106 us: shards(): total = lax.psum(limit.astype(jnp.float32), ('row', 'col', 'comp'))]
    pallas_call x0 -> x1, Pallas kernels: none -> 53.1 us  [shards(): pl.pallas_call(kernel, out_shape=jax.ShapeDtypeStruct((GROUP, 16, DIM), B...]
    dot_general x11 -> x0, matrix products: 24.1 us -> none  [the longest x9 9.39 us: conv_block(): jnp.dot(window, conv_weight[offset_row, offset_col], preferred_element_ty...]
    all_gather x3 -> x0, blocking collectives: 20.7 us -> none  [the longest x2 13.8 us: joined(): everything = jax.tree.map(lambda part: lax.all_gather(part, axis), x)]
    concatenate x3 -> x0, other arithmetic: 8.69 us -> none  [the longest x2 7.05 us: padded_2(): jnp.concatenate([lax.ppermute(tail, axis, [(i, (i + 1) % count) for i in...]
    reduce_sum x4 -> x0, other arithmetic: 7.53 us -> none  [the longest x1 4.91 us: moments(): return (stats, jnp.sum(gamma.astype(jnp.float32), axis=0))]
    ppermute x4 -> x0, starting transfers between devices: 7.44 us -> none  [the longest x2 4.86 us: padded_2(): lax.ppermute(tail, axis, [(i, (i + 1) % count) for i in range(ends)])]
  transfers between devices with their start and end apart: 6 -> 0, of which waited for: 3 -> 0; matrix products, arithmetic and copies ran while one was open for 2% -> 0% of each run, Pallas kernels for 0% -> 0%
where the time goes in v1:
time: 62.1 us; the launch traced here: 61.8 us
  Pallas kernels  53.1 us (86%)
  local copies, waits for them, and re-layouts  7.34 us (12%)
  between operations  1.31 us (2%)
    pallas_call x1, Pallas kernels, shards(): pl.pallas_call(kernel, out_shape=jax.ShapeDtypeStruct((GROUP, 16, DIM), B...  53.1 us
    unnamed x12, local copies, waits for them, and re-layouts  6.51 us

profile of v1, /device:TPU:0, one launch (start us, length us, event | category | flops | bytes accessed | tf_op | source)
XLA Modules:
  0.0 61.8 jit_solution(8314379114273521173)
XLA Ops:
  1.3 0.0 copy-start
  1.3 1.7 %copy-done = bf16[3,3,512,256]{3,2,1,0:T(8,128)(2,1)S(1)} copy-done((bf16[3,3,512,256]{3,2,1,0:T(8,128)(2,1)S(1)}, bf16[3,3,512,256]{3,2,1,0:T(8,128)(2,1)}, u32[]{:S(2)}) %copy-start) | copy-done | bytes 2359320
  2.9 0.0 copy-start.1
  2.9 1.6 %copy-done.1 = bf16[32,64,512]{2,1,0:T(8,128)(2,1)S(1)} copy-done((bf16[32,64,512]{2,1,0:T(8,128)(2,1)S(1)}, bf16[32,64,512]{2,1,0:T(8,128)(2,1)}, u32[]{:S(2)}) %copy-start.1) | copy-done | bytes 2097176
  4.5 0.0 copy-start.2
  4.5 0.9 %copy-done.2 = f32[256,256]{1,0:T(8,128)S(1)} copy-done((f32[256,256]{1,0:T(8,128)S(1)}, f32[256,256]{1,0:T(8,128)}, u32[]{:S(2)}) %copy-start.2) | copy-done | bytes 262168
  5.5 0.0 copy-start.3
  5.5 0.9 %copy-done.3 = f32[256,256]{1,0:T(8,128)S(1)} copy-done((f32[256,256]{1,0:T(8,128)S(1)}, f32[256,256]{1,0:T(8,128)}, u32[]{:S(2)}) %copy-start.3) | copy-done | bytes 262168
  6.4 0.0 copy-start.4
  6.4 0.7 %copy-done.4 = f32[1024]{0:T(1024)S(1)} copy-done((f32[1024]{0:T(1024)S(1)}, f32[1024]{0:T(1024)}, u32[]{:S(2)}) %copy-start.4) | copy-done | bytes 4120
  7.1 0.0 copy-start.5
  7.1 0.7 %copy-done.5 = f32[256]{0:T(256)S(1)} copy-done((f32[256]{0:T(256)S(1)}, f32[256]{0:T(256)}, u32[]{:S(2)}) %copy-start.5) | copy-done | bytes 1048
  7.8 53.1 %shard_map.86 = bf16[32,16,256]{2,1,0:T(8,128)(2,1)S(1)} custom-call(bf16[32,64,512]{2,1,0:T(8,128)(2,1)S(1)} %copy-done.1, bf16[3,3,512,256]{3,2,1,0:T(8,128)(2,1)S(1)} %copy-done, f32[1,256]{1,0:T(1,128)S(1)} %bitcast.7, f32[256,256]{1,0:T(8,128)S(1)} %copy-done.2, f32[256,256]{1,0:T(8,128)S(1)} %copy-done.3, f32[8,1,128]{2,1,0:T(1,128)S(1)} %bitcast.6, ...), custom_call_target="tpu_custom_call" | custom-call | tf_op jit(solution)/shard_map/pallas_call | solution.py:312
  61.0 0.8 %slice_bitcast_fusion = (f32[256,256]{1,0:T(8,128)}, f32[256,256]{1,0:T(8,128)}) fusion(f32[32,16,256]{2,1,0:T(8,128)S(1)} %convert_element_type.3), kind=kLoop, calls=%fused_computation | loop fusion | bytes 1048576 | tf_op jit(solution)/shard_map/reshape | solution.py:346
  (1 shorter events, 0.0 us)
Async XLA Ops:
  1.3 1.7 %copy-start = (bf16[3,3,512,256]{3,2,1,0:T(8,128)(2,1)S(1)}, bf16[3,3,512,256]{3,2,1,0:T(8,128)(2,1)}, u32[]{:S(2)}) copy-start(bf16[3,3,512,256]{3,2,1,0:T(8,128)(2,1)} %conv_weight.1) | copy-start | bytes 7077892
  2.9 1.6 %copy-start.1 = (bf16[32,64,512]{2,1,0:T(8,128)(2,1)S(1)}, bf16[32,64,512]{2,1,0:T(8,128)(2,1)}, u32[]{:S(2)}) copy-start(bf16[32,64,512]{2,1,0:T(8,128)(2,1)} %features.1) | copy-start | bytes 6291460
  4.5 0.9 %copy-start.2 = (f32[256,256]{1,0:T(8,128)S(1)}, f32[256,256]{1,0:T(8,128)}, u32[]{:S(2)}) copy-start(f32[256,256]{1,0:T(8,128)} %means.1) | copy-start | bytes 786436
  5.5 0.9 %copy-start.3 = (f32[256,256]{1,0:T(8,128)S(1)}, f32[256,256]{1,0:T(8,128)}, u32[]{:S(2)}) copy-start(f32[256,256]{1,0:T(8,128)} %precisions.1) | copy-start | bytes 786436
  6.4 0.7 %copy-start.4 = (f32[1024]{0:T(1024)S(1)}, f32[1024]{0:T(1024)}, u32[]{:S(2)}) copy-start(f32[1024]{0:T(1024)} %param.12) | copy-start | bytes 12292
  7.1 0.7 %copy-start.5 = (f32[256]{0:T(256)S(1)}, f32[256]{0:T(256)}, u32[]{:S(2)}) copy-start(f32[256]{0:T(256)} %param.9) | copy-start | bytes 3076

commit v2 on v1

v2 whole, which is shorter than its diff:
```python
import functools

import jax
import jax.numpy as jnp
from jax import lax
from jax.experimental import pallas as pl
from jax.experimental.pallas import tpu as pltpu
from jax.sharding import PartitionSpec as P

F32 = jnp.float32
BF16 = jnp.bfloat16
MESH = pl.DeviceIdType.MESH

HEIGHT, WIDTH, CHAN, DIM = 32, 64, 512, 256
COMPS, BLOCK = 1024, 256
PATCHES = HEIGHT * WIDTH
CHUNK = 512
ROWS = CHUNK // WIDTH
CHIPS = 64
GROUP = 32
PIECES = 4


def signal(sem, device):
    pl.semaphore_signal(sem, inc=1, device_id=device, device_id_type=MESH)


def remote(src, dst, send_sem, recv_sem, device):
    return pltpu.make_async_remote_copy(
        src_ref=src, dst_ref=dst, send_sem=send_sem, recv_sem=recv_sem,
        device_id=device, device_id_type=MESH,
    )


def column(line):
    return jnp.broadcast_to(line, (128, 128)).T


def kernel(
    features, conv_weight, bias_in, means_in, precisions_in, logits_in, count_in, out,
    x, w, bias, logits, count, means, precisions, ends, raw, sides, corners, edge, panel, offset_lines, offsets,
    own_logs, design, mass, gamma, zeroth, give, take, held, landed, gathered,
    sums_give, sums_take, sums_held, sums_landed, sums_column,
    load_sem, halo_send, halo_recv, panel_send, panel_recv, pair_send, pair_recv,
    sums_pair, scatter_send, scatter_recv, sums_send, sums_recv, gather_send, gather_recv, heard,
):
    row, col, comp = lax.axis_index("row"), lax.axis_index("col"), lax.axis_index("comp")
    core = lax.rem(comp, 2)
    upper = comp // 2
    tile = col * 4 + comp
    me = row * 8 + col * 2 + upper
    partner = (row, col, comp + 1 - 2 * core)
    across = (row + 1 - 2 * lax.rem(row, 2), col, lax.rem(comp + 2, 4))

    def chip(number):
        return (number // 8, lax.rem(number // 2, 4), 2 * lax.rem(number, 2) + core)

    def spot(down, right):
        there = tile + right
        return (row + down, there // 4, lax.rem(there, 4))

    def exists(down, right):
        ok = jnp.bool_(True)
        if down < 0:
            ok = row > 0
        if down > 0:
            ok = row < 7
        if right < 0:
            ok = jnp.logical_and(ok, tile > 0)
        if right > 0:
            ok = jnp.logical_and(ok, tile < 15)
        return ok

    loads = [
        pltpu.make_async_copy(src, dst, load_sem.at[k])
        for k, (src, dst) in enumerate((
            (means_in, means), (precisions_in, precisions), (features, x.at[pl.ds(1, HEIGHT)]), (logits_in, logits),
            (bias_in, bias), (count_in, count), (conv_weight, w),
        ))
    ]
    for load in loads:
        load.start()

    barrier = pltpu.get_barrier_semaphore()
    lower = lax.rem(row, 2)
    z_peers = [(row, lax.rem(col + k, 4), comp) for k in (1, 2, 3)]
    x_peers = [(lax.rem(row + 2 * k, 8), col, comp) for k in (1, 2, 3)]
    y_peers = [
        (row + 1 - 2 * lower, col, comp),
        (row, col, lax.rem(comp + 2, 4)),
        across,
    ]
    around = [(-1, 0), (1, 0), (0, -1), (0, 1), (-1, -1), (-1, 1), (1, -1), (1, 1)]
    for device in y_peers + [partner] + x_peers + z_peers:
        signal(barrier, device)
    greeted = 10
    for place in around:
        @pl.when(exists(*place))
        def _():
            signal(barrier, spot(*place))
        greeted = greeted + exists(*place).astype(jnp.int32)

    loads[0].wait()
    loads[1].wait()
    centres = means[...]
    inverse = precisions[...]
    panel[comp] = jnp.concatenate(
        [(centres * inverse).astype(BF16), (-0.5 * inverse).astype(BF16)], axis=1
    )
    pl.semaphore_wait(barrier, greeted)

    def hear(peers, k):
        for device in peers:
            signal(heard.at[k], device)

    far = lax.rem(comp + 2, 4)
    beyond = far + 1 - 2 * core

    def panel_copy(block, piece, slot, device):
        rows = panel.at[block, pl.ds(piece * (BLOCK // PIECES), BLOCK // PIECES)]
        return remote(rows, rows, panel_send.at[slot, piece], panel_recv.at[slot, piece], device)

    def offset_copy(block, slot, device):
        lines = offset_lines.at[block]
        return remote(lines, lines, panel_send.at[slot, PIECES], panel_recv.at[slot, PIECES], device)

    to_across = [panel_copy(comp, piece, 0, across) for piece in range(PIECES)]
    to_partner = [panel_copy(comp, piece, 1, partner) for piece in range(PIECES)]
    onward = [panel_copy(far, piece, 2, partner) for piece in range(PIECES)]
    offsets_across, offsets_partner, offsets_onward = (
        offset_copy(comp, 0, across), offset_copy(comp, 1, partner), offset_copy(far, 2, partner)
    )
    for copy in to_across + to_partner:
        copy.start()
    hear(x_peers, 0)

    loads[2].wait()
    halos = []

    def halo(index, down, right, src, dst):
        halos.append((index, down, right, remote(src, dst, halo_send.at[index], halo_recv.at[index], spot(down, right))))
        @pl.when(exists(down, right))
        def _():
            halos[-1][3].start()

    halo(0, -1, 0, x.at[1], ends.at[1])
    halo(1, 1, 0, x.at[HEIGHT], ends.at[0])
    halo(2, -1, -1, x.at[1, pl.ds(0, 16)], corners.at[1, 1])
    halo(3, -1, 1, x.at[1, pl.ds(WIDTH - 16, 16)], corners.at[0, 1])
    halo(4, 1, -1, x.at[HEIGHT, pl.ds(0, 16)], corners.at[1, 0])
    halo(5, 1, 1, x.at[HEIGHT, pl.ds(WIDTH - 16, 16)], corners.at[0, 0])
    flat = x[1 : HEIGHT + 1].reshape(PATCHES, CHAN)
    line = lax.broadcasted_iota(jnp.int32, (2 * HEIGHT, PATCHES), 0)
    patch = lax.broadcasted_iota(jnp.int32, (2 * HEIGHT, PATCHES), 1)
    wanted = jnp.where(line < HEIGHT, line * WIDTH, (line - HEIGHT) * WIDTH + WIDTH - 1)
    picked = jnp.dot(
        jnp.where(patch == wanted, 1.0, 0.0).astype(BF16), flat, preferred_element_type=F32
    ).astype(BF16)
    edge[0] = picked[:HEIGHT]
    edge[1] = picked[HEIGHT:]
    halo(6, 0, -1, edge.at[0], sides.at[1])
    halo(7, 0, 1, edge.at[1], sides.at[0])

    loads[3].wait()
    lines = logits[...]
    top = jnp.max(jnp.max(lines, axis=0), axis=1, keepdims=True)
    norm = top + jnp.log(jnp.sum(jnp.sum(jnp.exp(lines - top[None]), axis=0), axis=1, keepdims=True))
    logs = jnp.concatenate([column(logits[2 * comp] - norm), column(logits[2 * comp + 1] - norm)], axis=0)
    own_logs[...] = logs
    constant = 0.5 * jnp.sum(jnp.log(inverse), axis=1, keepdims=True) - 0.5 * jnp.sum(
        inverse * centres * centres, axis=1, keepdims=True
    )
    own_offset = logs + constant
    for half in range(2):
        offset_lines[comp, half] = own_offset[half * 128 : half * 128 + 128].T[:8]
    offsets_across.start()
    offsets_partner.start()

    x[0] = jnp.zeros((WIDTH, CHAN), BF16)
    x[HEIGHT + 1] = jnp.zeros((WIDTH, CHAN), BF16)

    @pl.when(row == 0)
    def _():
        ends[0] = jnp.zeros((WIDTH, CHAN), BF16)

    @pl.when(row == 7)
    def _():
        ends[1] = jnp.zeros((WIDTH, CHAN), BF16)

    for side, edge_tile in ((0, 0), (1, 15)):
        @pl.when(tile == edge_tile)
        def _():
            sides[side] = jnp.zeros((HEIGHT, CHAN), BF16)

        for end, edge_row in ((0, 0), (1, 7)):
            @pl.when(jnp.logical_or(tile == edge_tile, row == edge_row))
            def _():
                corners[side, end] = jnp.zeros((16, CHAN), BF16)

    for load in loads[4:]:
        load.wait()

    def shifted(y, height):
        c = lax.broadcasted_iota(jnp.int32, (height, WIDTH, DIM), 1)
        count = height * WIDTH
        before = jnp.where(c == 0, 0.0, pltpu.roll(y[0], 1, 0).reshape(height, WIDTH, DIM))
        after = jnp.where(c == WIDTH - 1, 0.0, pltpu.roll(y[2], count - 1, 0).reshape(height, WIDTH, DIM))
        return y[1].reshape(height, WIDTH, DIM) + before + after

    def convolve(i):
        lhs = jnp.concatenate(
            [x[i * ROWS + k : i * ROWS + k + ROWS].reshape(CHUNK, CHAN) for k in range(3)], axis=1
        )
        y = [
            jnp.dot(lhs, w[:, tap].reshape(3 * CHAN, DIM), preferred_element_type=F32)
            for tap in range(3)
        ]
        raw[i * ROWS : (i + 1) * ROWS] = shifted(y, ROWS) + bias[...].reshape(1, 1, DIM)

    for i in range(PATCHES // CHUNK):
        convolve(i)

    pl.semaphore_wait(heard.at[0], 3)
    hear(y_peers, 1)
    for index, down, right, copy in halos:
        @pl.when(exists(down, right))
        def _():
            copy.wait_send()

        @pl.when(exists(-down, -right))
        def _():
            copy.wait_recv()

    beside = [jnp.concatenate([sides[side], corners[side, 0], corners[side, 1]], axis=0) for side in range(2)]
    products = {}
    for k in range(3):
        for tap in range(3):
            lhs = []
            if k != 1:
                lhs.append(ends[k // 2])
            if tap != 1:
                lhs.append(beside[tap // 2])
            if lhs:
                products[k, tap] = jnp.dot(
                    lhs[0] if len(lhs) == 1 else jnp.concatenate(lhs, axis=0), w[k, tap], preferred_element_type=F32
                )
    for k, at in ((0, 0), (2, HEIGHT - 1)):
        raw[at] += shifted([products[k, tap][:WIDTH] for tap in range(3)], 1)[0]
    r = lax.broadcasted_iota(jnp.int32, (HEIGHT, DIM), 0)
    c = lax.broadcasted_iota(jnp.int32, (HEIGHT, 8, DIM), 1)
    for side, tap, at in ((0, 0, 15), (1, 2, 0)):
        y = [products[k, tap][-WIDTH:] for k in range(3)]
        above = jnp.where(r == 0, y[0][32 + at : 33 + at], pltpu.roll(y[0][:HEIGHT], 1, 0))
        below = jnp.where(r == HEIGHT - 1, y[2][48 + at : 49 + at], pltpu.roll(y[2][:HEIGHT], HEIGHT - 1, 0))
        more = (above + y[1][:HEIGHT] + below).reshape(HEIGHT, 1, DIM)
        if side == 0:
            raw[:, :8] += jnp.where(c == 0, more, 0.0)
        else:
            raw[:, WIDTH - 8 :] += jnp.where(c == 7, more, 0.0)

    for i in range(PATCHES // CHUNK):
        encoded = raw[i * ROWS : (i + 1) * ROWS].reshape(CHUNK, DIM).astype(BF16)
        wide = encoded.astype(F32)
        design[i * CHUNK : (i + 1) * CHUNK, :DIM] = encoded
        design[i * CHUNK : (i + 1) * CHUNK, DIM:] = (wide * wide).astype(BF16)

    offsets_across.wait()
    offsets_onward.start()
    for piece in range(2):
        to_across[piece].wait()
        onward[piece].start()

    for copy in to_partner + [offsets_partner]:
        copy.wait()

    def score(i, first, second):
        flipped = design[i * CHUNK : (i + 1) * CHUNK, :DIM].T
        wide = flipped.astype(F32)
        rhs = jnp.concatenate([flipped, (wide * wide).astype(BF16)], axis=0)
        lhs = jnp.concatenate([panel[first], panel[second]], axis=0)
        add = jnp.concatenate([offsets[first], offsets[second]], axis=0)
        scores = jnp.dot(lhs, rhs, preferred_element_type=F32) + jnp.concatenate([add] * (CHUNK // 128), axis=1)
        peak = jnp.max(scores, axis=0, keepdims=True)
        grown = jnp.exp(scores - peak)
        return peak, grown, jnp.sum(grown, axis=0, keepdims=True)

    def spread_offsets(block):
        for half in range(2):
            offsets[block, half * 128 : half * 128 + 128] = column(offset_lines[block, half, :1])

    spread_offsets(comp)
    spread_offsets(comp + 1 - 2 * core)
    near = []
    for i in range(PATCHES // CHUNK):
        peak, grown, total = score(i, comp, comp + 1 - 2 * core)
        mass[:, i * CHUNK : (i + 1) * CHUNK] = grown
        near.append((peak, total))

    for piece in range(2, PIECES):
        to_across[piece].wait()
        onward[piece].start()
    for copy in [offsets_onward] + onward:
        copy.wait()
    spread_offsets(far)
    spread_offsets(beyond)
    limit = count[...]
    for i in range(PATCHES // CHUNK):
        at = slice(i * CHUNK, (i + 1) * CHUNK)
        peak, grown, total = score(i, far, beyond)
        near_peak, near_total = near[i]
        top = jnp.maximum(peak, near_peak)
        lift, near_lift = jnp.exp(peak - top), jnp.exp(near_peak - top)
        where = lax.broadcasted_iota(jnp.int32, (1, CHUNK), 1) + i * CHUNK
        scale = jnp.where(where < limit, 1.0 / (total * lift + near_total * near_lift), 0.0)
        for k, weight in ((0, mass[:, at] * (scale * near_lift)), (1, grown * (scale * lift))):
            rows = slice(k * 512, (k + 1) * 512)
            weight = weight.astype(BF16)
            gamma[rows, at] = weight
            weight = weight.astype(F32)
            part = weight[:, :128]
            for m in range(1, CHUNK // 128):
                part = part + weight[:, m * 128 : m * 128 + 128]
            if i == 0:
                zeroth[rows] = part
            else:
                zeroth[rows] += part

    pl.semaphore_wait(heard.at[1], 3)

    tally = jnp.broadcast_to(limit.astype(F32), (1, 128))
    for h, order in ((0, 0), (1, 2)):
        for half in range(2):
            for ref, place in ((sums_held, order), (sums_give, order + 1)):
                start = place * BLOCK + half * 128
                ref[h, half, 0] = jnp.sum(zeroth[start : start + 128].T, axis=0, keepdims=True)
                ref[h, half, 1] = tally
    sums_copy = remote(sums_give, sums_take, sums_pair.at[0], sums_pair.at[1], partner)
    sums_copy.start()

    def statistics(place):
        stats = jnp.dot(gamma[place * BLOCK : (place + 1) * BLOCK, :], design[...], preferred_element_type=F32)
        return jnp.concatenate(
            [stats[:, :DIM].reshape(GROUP, 8, DIM), stats[:, DIM:].reshape(GROUP, 8, DIM)], axis=1
        )

    pair = []
    for k in range(2):
        give[k] = statistics(2 * k + 1).astype(BF16)
        pair.append(remote(give.at[k], take.at[k], pair_send.at[k], pair_recv.at[k], partner))
        pair[k].start()

    sums_copy.wait()
    sums_held[...] += sums_take[...]

    def scatter(k):
        def send(step, carry):
            step = 2 * step + k
            to = lax.rem(me + step, CHIPS)
            remote(held.at[k, to // 2], landed.at[CHIPS - step], scatter_send, scatter_recv, chip(to)).start()
            return carry

        lax.fori_loop(1 - k, GROUP, send, 0)

    def scatter_sums(step, carry):
        to = lax.rem(me + step, CHIPS)
        away = lax.rem(lax.rem(to, 2) + upper, 2)
        remote(
            sums_held.at[away, to // 32], sums_landed.at[CHIPS - step], sums_send, sums_recv, chip(to)
        ).start()
        return carry

    for k in range(2):
        mine = statistics(2 * k)
        pair[k].wait()
        held[k] = (mine + take[k].astype(F32)).astype(BF16)
        scatter(k)
        if k == 0:
            lax.fori_loop(1, CHIPS, scatter_sums, 0)

    owner = row * 4 + col
    landed[0] = held[0, owner]
    sums_landed[0] = sums_held[0, owner // 16]
    for buffer, send, recv in ((sums_landed, sums_send, sums_recv), (landed, scatter_send, scatter_recv)):
        all_but_own = buffer.at[pl.ds(1, CHIPS - 1)]
        everyone = remote(all_but_own, all_but_own, send, recv, partner)
        everyone.wait_send()
        everyone.wait_recv()
    sums = jnp.sum(sums_landed[...], axis=0)
    sums_column[...] = column(sums[0])
    patches = sums[1][:, :1]
    total = jnp.sum(landed[...].astype(F32), axis=0)
    first = total[:8]
    second = total[8:]
    amount = sums_column[pl.ds(pl.multiple_of(lax.rem(owner, 16) * 8, 8), 8), :]
    amount = jnp.concatenate([amount, amount], axis=1)
    rows = pl.ds(pl.multiple_of(owner * 8, 8), 8)
    centre = means[rows, :]
    inverse = precisions[rows, :]
    share = jnp.exp(own_logs[rows, :1])
    mean_fisher = (first - centre * amount) * jnp.sqrt(inverse) / jnp.sqrt(patches * share)
    var_fisher = (
        second * inverse - 2.0 * centre * inverse * first + (centre * centre * inverse - 1.0) * amount
    ) / jnp.sqrt(2.0 * patches * share)
    gathered[owner] = jnp.concatenate([mean_fisher, var_fisher], axis=0).astype(BF16)

    def gather(step, carry):
        to = lax.rem(owner + step, GROUP)
        remote(
            gathered.at[owner], gathered.at[owner], gather_send, gather_recv, (to // 4, lax.rem(to, 4), comp)
        ).start()
        return carry

    lax.fori_loop(1, GROUP, gather, 0)
    others = remote(gathered.at[pl.ds(1, GROUP - 1)], gathered.at[pl.ds(1, GROUP - 1)], gather_send, gather_recv, partner)
    others.wait_send()
    others.wait_recv()
    out[...] = gathered[...]


def shards(features, conv_weight, conv_bias, means, precisions, mix_logits, tissue_counts):
    vmem = pl.BlockSpec(memory_space=pltpu.VMEM)
    hbm = pl.BlockSpec(memory_space=pltpu.HBM)
    dma = pltpu.SemaphoreType.DMA
    fisher = pl.pallas_call(
        kernel,
        out_shape=jax.ShapeDtypeStruct((GROUP, 16, DIM), BF16),
        in_specs=[hbm] * 7,
        out_specs=vmem,
        scratch_shapes=[
            pltpu.VMEM((HEIGHT + 2, WIDTH, CHAN), BF16),
            pltpu.VMEM((3, 3, CHAN, DIM), BF16),
            pltpu.VMEM((1, DIM), F32),
            pltpu.VMEM((8, 1, 128), F32),
            pltpu.VMEM((1, 1), jnp.int32),
            pltpu.VMEM((BLOCK, DIM), F32),
            pltpu.VMEM((BLOCK, DIM), F32),
            pltpu.VMEM((2, WIDTH, CHAN), BF16),
            pltpu.VMEM((HEIGHT, WIDTH, DIM), F32),
            pltpu.VMEM((2, HEIGHT, CHAN), BF16),
            pltpu.VMEM((2, 2, 16, CHAN), BF16),
            pltpu.VMEM((2, HEIGHT, CHAN), BF16),
            pltpu.VMEM((4, BLOCK, 2 * DIM), BF16),
            pltpu.VMEM((4, 2, 8, 128), F32),
            pltpu.VMEM((4, BLOCK, 128), F32),
            pltpu.VMEM((BLOCK, 128), F32),
            pltpu.VMEM((PATCHES, 2 * DIM), BF16),
            pltpu.VMEM((COMPS // 2, PATCHES), F32),
            pltpu.VMEM((COMPS, PATCHES), BF16),
            pltpu.VMEM((COMPS, 128), F32),
            pltpu.VMEM((2, GROUP, 16, DIM), BF16),
            pltpu.VMEM((2, GROUP, 16, DIM), BF16),
            pltpu.VMEM((2, GROUP, 16, DIM), BF16),
            pltpu.VMEM((CHIPS, 16, DIM), BF16),
            pltpu.VMEM((GROUP, 16, DIM), BF16),
            pltpu.VMEM((2, 2, 2, 1, 128), F32),
            pltpu.VMEM((2, 2, 2, 1, 128), F32),
            pltpu.VMEM((2, 2, 2, 1, 128), F32),
            pltpu.VMEM((CHIPS, 2, 1, 128), F32),
            pltpu.VMEM((128, 128), F32),
            dma((7,)), dma((8,)), dma((8,)), dma((3, PIECES + 1)), dma((3, PIECES + 1)), dma((2,)), dma((2,)),
            dma((2,)), dma, dma, dma, dma, dma, dma, pltpu.SemaphoreType.REGULAR((2,)),
        ],
        compiler_params=pltpu.CompilerParams(
            collective_id=0, has_side_effects=True, vmem_limit_bytes=56 * 2**20
        ),
    )(
        features, conv_weight, conv_bias.reshape(1, DIM), means, precisions,
        mix_logits.reshape(8, 1, 128), tissue_counts,
    )
    return tuple(
        fisher[:, 8 * k : 8 * k + 8].astype(F32).reshape(BLOCK, DIM) for k in range(2)
    )


def solution(mesh):
    in_specs = (
        P("row", ("col", "comp"), None),
        P(),
        P(),
        P("comp", None),
        P("comp", None),
        P(),
        P("row", ("col", "comp")),
    )
    out_specs = (P("comp", None), P("comp", None))
    return jax.shard_map(shards, mesh=mesh, in_specs=in_specs, out_specs=out_specs, check_vma=False)
```

time: 62.1 us -> 51.1 us (0.82)
  local copies, waits for them, and re-layouts: 7.34 us -> 0 us
  Pallas kernels: 53.1 us -> 47.6 us
  other arithmetic: 0.05 us -> 1.79 us
    unnamed x12 -> x0, local copies, waits for them, and re-layouts: 6.51 us -> none
    pallas_call x1, Pallas kernels: 53.1 us -> 47.6 us  [shards(): pl.pallas_call(kernel, out_shape=jax.ShapeDtypeStruct((GROUP, 16, DIM), B...]
    reshape x0 -> x1, other arithmetic: none -> 1.79 us  [shards(): fisher[:, 8 * k:8 * k + 8].astype(F32).reshape(BLOCK, DIM)]
    reshape x1 -> x0, local copies, waits for them, and re-layouts: 0.83 us -> none  [shards(): fisher[:, 8:].reshape(BLOCK, DIM)]
where the time goes in v2:
time: 51.1 us; the launch traced here: 50.7 us
  Pallas kernels  47.6 us (93%)
  other arithmetic  1.79 us (4%)
  between operations  1.29 us (3%)
    pallas_call x1, Pallas kernels, shards(): pl.pallas_call(kernel, out_shape=jax.ShapeDtypeStruct((GROUP, 16, DIM), B...  47.6 us
    reshape x1, other arithmetic, shards(): fisher[:, 8 * k:8 * k + 8].astype(F32).reshape(BLOCK, DIM)  1.79 us

profile of v2, /device:TPU:0, one launch (start us, length us, event | category | flops | bytes accessed | tf_op | source)
XLA Modules:
  0.0 50.7 jit_solution(5224789016381790209)
XLA Ops:
  1.3 47.6 %shard_map.86 = bf16[32,16,256]{2,1,0:T(8,128)(2,1)} custom-call(bf16[32,64,512]{2,1,0:T(8,128)(2,1)} %features.1, bf16[3,3,512,256]{3,2,1,0:T(8,128)(2,1)} %conv_weight.1, f32[1,256]{1,0:T(1,128)} %bitcast.9, f32[256,256]{1,0:T(8,128)} %means_in.1, f32[256,256]{1,0:T(8,128)} %precisions_in.1, f32[8,1,128]{2,1,0:T(1,128)} %bitcast.8, s32[1,1]{1,0:T(1,128)S(6)} %copy.9.count_in), custom_call_target="tpu_custom_call" | custom-call | tf_op jit(solution)/shard_map/pallas_call | solution.py:424
  48.9 1.8 %bitcast_convert_fusion = (f32[256,256]{1,0:T(8,128)}, f32[256,256]{1,0:T(8,128)}) fusion(bf16[32,16,256]{2,1,0:T(8,128)(2,1)} %shard_map.86), kind=kLoop, calls=%fused_computation | loop fusion | flops 131072 | bytes 786432 | tf_op jit(solution)/shard_map/reshape | solution.py:471

commit v3 on v2

--- a/solution.py
+++ b/solution.py
@@ -38,11 +38,11 @@
 
 def kernel(
     features, conv_weight, bias_in, means_in, precisions_in, logits_in, count_in, out,
-    x, w, bias, logits, count, means, precisions, ends, raw, sides, corners, edge, panel, offset_lines, offsets,
+    x, w, bias, logits, count, means, precisions, ends, raw, sides, corners, corners_out, edge, panel, offset_lines, offsets,
     own_logs, design, mass, gamma, zeroth, give, take, held, landed, gathered,
-    sums_give, sums_take, sums_held, sums_landed, sums_column,
+    sums_give, sums_take, sums_held, sums_landed, sums_total, sums_column,
     load_sem, halo_send, halo_recv, panel_send, panel_recv, pair_send, pair_recv,
-    sums_pair, scatter_send, scatter_recv, sums_send, sums_recv, gather_send, gather_recv, heard,
+    sums_pair, scatter_send, scatter_recv, sums_send, sums_recv, gather_send, gather_recv, total_send, total_recv, heard,
 ):
     row, col, comp = lax.axis_index("row"), lax.axis_index("col"), lax.axis_index("comp")
     core = lax.rem(comp, 2)
@@ -145,10 +145,6 @@
 
     halo(0, -1, 0, x.at[1], ends.at[1])
     halo(1, 1, 0, x.at[HEIGHT], ends.at[0])
-    halo(2, -1, -1, x.at[1, pl.ds(0, 16)], corners.at[1, 1])
-    halo(3, -1, 1, x.at[1, pl.ds(WIDTH - 16, 16)], corners.at[0, 1])
-    halo(4, 1, -1, x.at[HEIGHT, pl.ds(0, 16)], corners.at[1, 0])
-    halo(5, 1, 1, x.at[HEIGHT, pl.ds(WIDTH - 16, 16)], corners.at[0, 0])
     flat = x[1 : HEIGHT + 1].reshape(PATCHES, CHAN)
     line = lax.broadcasted_iota(jnp.int32, (2 * HEIGHT, PATCHES), 0)
     patch = lax.broadcasted_iota(jnp.int32, (2 * HEIGHT, PATCHES), 1)
@@ -160,6 +156,15 @@
     edge[1] = picked[HEIGHT:]
     halo(6, 0, -1, edge.at[0], sides.at[1])
     halo(7, 0, 1, edge.at[1], sides.at[0])
+    for index, down, right in ((2, -1, -1), (3, -1, 1), (4, 1, -1), (5, 1, 1)):
+        side, end = (1 - right) // 2, (1 - down) // 2
+        k = 0 if down < 0 else HEIGHT - 1
+        spread = picked[(1 - side) * HEIGHT + k : (1 - side) * HEIGHT + k + 1].astype(F32)
+        spread = jnp.concatenate(
+            [spread[:, 128 * q : 128 * q + 128] for q in range(4)] + [jnp.zeros((12, 128), F32)], axis=0
+        )
+        corners_out[side, end] = spread.astype(BF16)
+        halo(index, down, right, corners_out.at[side, end], corners.at[side, end])
 
     loads[3].wait()
     lines = logits[...]
@@ -195,7 +200,7 @@
         for end, edge_row in ((0, 0), (1, 7)):
             @pl.when(jnp.logical_or(tile == edge_tile, row == edge_row))
             def _():
-                corners[side, end] = jnp.zeros((16, CHAN), BF16)
+                corners[side, end] = jnp.zeros((16, 128), BF16)
 
     for load in loads[4:]:
         load.wait()
@@ -231,7 +236,12 @@
         def _():
             copy.wait_recv()
 
-    beside = [jnp.concatenate([sides[side], corners[side, 0], corners[side, 1]], axis=0) for side in range(2)]
+    def corner(side, end):
+        tile_of = corners[side, end].astype(F32)
+        line = jnp.concatenate([tile_of[q : q + 1] for q in range(4)], axis=1)
+        return jnp.broadcast_to(line, (16, CHAN)).astype(BF16)
+
+    beside = [jnp.concatenate([sides[side], corner(side, 0), corner(side, 1)], axis=0) for side in range(2)]
     products = {}
     for k in range(3):
         for tap in range(3):
@@ -248,10 +258,10 @@
         raw[at] += shifted([products[k, tap][:WIDTH] for tap in range(3)], 1)[0]
     r = lax.broadcasted_iota(jnp.int32, (HEIGHT, DIM), 0)
     c = lax.broadcasted_iota(jnp.int32, (HEIGHT, 8, DIM), 1)
-    for side, tap, at in ((0, 0, 15), (1, 2, 0)):
+    for side, tap in ((0, 0), (1, 2)):
         y = [products[k, tap][-WIDTH:] for k in range(3)]
-        above = jnp.where(r == 0, y[0][32 + at : 33 + at], pltpu.roll(y[0][:HEIGHT], 1, 0))
-        below = jnp.where(r == HEIGHT - 1, y[2][48 + at : 49 + at], pltpu.roll(y[2][:HEIGHT], HEIGHT - 1, 0))
+        above = jnp.where(r == 0, y[0][32:33], pltpu.roll(y[0][:HEIGHT], 1, 0))
+        below = jnp.where(r == HEIGHT - 1, y[2][48:49], pltpu.roll(y[2][:HEIGHT], HEIGHT - 1, 0))
         more = (above + y[1][:HEIGHT] + below).reshape(HEIGHT, 1, DIM)
         if side == 0:
             raw[:, :8] += jnp.where(c == 0, more, 0.0)
@@ -263,12 +273,6 @@
         wide = encoded.astype(F32)
         design[i * CHUNK : (i + 1) * CHUNK, :DIM] = encoded
         design[i * CHUNK : (i + 1) * CHUNK, DIM:] = (wide * wide).astype(BF16)
-
-    offsets_across.wait()
-    offsets_onward.start()
-    for piece in range(2):
-        to_across[piece].wait()
-        onward[piece].start()
 
     for copy in to_partner + [offsets_partner]:
         copy.wait()
@@ -295,10 +299,14 @@
         peak, grown, total = score(i, comp, comp + 1 - 2 * core)
         mass[:, i * CHUNK : (i + 1) * CHUNK] = grown
         near.append((peak, total))
-
-    for piece in range(2, PIECES):
-        to_across[piece].wait()
-        onward[piece].start()
+        if i >= 1:
+            to_across[i - 1].wait()
+            onward[i - 1].start()
+
+    offsets_across.wait()
+    offsets_onward.start()
+    to_across[PIECES - 1].wait()
+    onward[PIECES - 1].start()
     for copy in [offsets_onward] + onward:
         copy.wait()
     spread_offsets(far)
@@ -361,43 +369,76 @@
 
         lax.fori_loop(1 - k, GROUP, send, 0)
 
-    def scatter_sums(step, carry):
-        to = lax.rem(me + step, CHIPS)
-        away = lax.rem(lax.rem(to, 2) + upper, 2)
-        remote(
-            sums_held.at[away, to // 32], sums_landed.at[CHIPS - step], sums_send, sums_recv, chip(to)
-        ).start()
-        return carry
+    owner = row * 4 + col
+    adds = lax.rem(owner, 16) == 5
+    lines_out = []
+    for h, block in ((0, comp), (1, far)):
+        for half in range(2):
+            to = (4 * half + 1) * 8 + 2 + block // 2
+            lines_out.append((to, remote(
+                sums_held.at[h, half], sums_landed.at[lax.rem(me - to + CHIPS, CHIPS)],
+                sums_send, sums_recv, (4 * half + 1, 1, block),
+            )))
+            @pl.when(to != me)
+            def _():
+                lines_out[-1][1].start()
 
     for k in range(2):
         mine = statistics(2 * k)
         pair[k].wait()
         held[k] = (mine + take[k].astype(F32)).astype(BF16)
         scatter(k)
-        if k == 0:
-            lax.fori_loop(1, CHIPS, scatter_sums, 0)
-
-    owner = row * 4 + col
+
     landed[0] = held[0, owner]
-    sums_landed[0] = sums_held[0, owner // 16]
-    for buffer, send, recv in ((sums_landed, sums_send, sums_recv), (landed, scatter_send, scatter_recv)):
-        all_but_own = buffer.at[pl.ds(1, CHIPS - 1)]
-        everyone = remote(all_but_own, all_but_own, send, recv, partner)
-        everyone.wait_send()
-        everyone.wait_recv()
-    sums = jnp.sum(sums_landed[...], axis=0)
+
+    def pass_on(step, carry):
+        to = owner // 16 * 16 + lax.rem(lax.rem(owner, 16) + step, 16)
+        remote(
+            sums_total, sums_total, total_send, total_recv, (to // 4, lax.rem(to, 4), comp)
+        ).start()
+        return carry
+
+    @pl.when(adds)
+    def _():
+        arrived = sums_landed.at[pl.ds(1, CHIPS - 1)]
+        sums_landed[0] = sums_held[0, owner // 16]
+        remote(arrived, arrived, sums_send, sums_recv, partner).wait_recv()
+        sums_total[...] = jnp.sum(sums_landed[...], axis=0)
+        lax.fori_loop(1, 16, pass_on, 0)
+
+    for to, copy in lines_out:
+        @pl.when(to != me)
+        def _():
+            copy.wait_send()
+
+    rows = pl.ds(pl.multiple_of(owner * 8, 8), 8)
+    centre = means[rows, :]
+    inverse = precisions[rows, :]
+    root = jnp.sqrt(inverse)
+    share = jnp.exp(own_logs[rows, :1])
+    all_but_own = landed.at[pl.ds(1, CHIPS - 1)]
+    everyone = remote(all_but_own, all_but_own, scatter_send, scatter_recv, partner)
+    everyone.wait_send()
+    everyone.wait_recv()
+    total = jnp.sum(landed[...].astype(F32), axis=0)
+
+    @pl.when(adds)
+    def _():
+        sent = sums_landed.at[pl.ds(0, 15)]
+        remote(sent, sent, total_send, total_recv, partner).wait_send()
+
+    @pl.when(jnp.logical_not(adds))
+    def _():
+        remote(sums_total, sums_total, total_send, total_recv, partner).wait_recv()
+
+    sums = sums_total[...]
     sums_column[...] = column(sums[0])
     patches = sums[1][:, :1]
-    total = jnp.sum(landed[...].astype(F32), axis=0)
     first = total[:8]
     second = total[8:]
     amount = sums_column[pl.ds(pl.multiple_of(lax.rem(owner, 16) * 8, 8), 8), :]
     amount = jnp.concatenate([amount, amount], axis=1)
-    rows = pl.ds(pl.multiple_of(owner * 8, 8), 8)
-    centre = means[rows, :]
-    inverse = precisions[rows, :]
-    share = jnp.exp(own_logs[rows, :1])
-    mean_fisher = (first - centre * amount) * jnp.sqrt(inverse) / jnp.sqrt(patches * share)
+    mean_fisher = (first - centre * amount) * root / jnp.sqrt(patches * share)
     var_fisher = (
         second * inverse - 2.0 * centre * inverse * first + (centre * centre * inverse - 1.0) * amount
     ) / jnp.sqrt(2.0 * patches * share)
@@ -423,7 +464,7 @@
     dma = pltpu.SemaphoreType.DMA
     fisher = pl.pallas_call(
         kernel,
-        out_shape=jax.ShapeDtypeStruct((GROUP, 16, DIM), BF16),
+        out_shape=pltpu.VMEM((GROUP, 16, DIM), BF16),
         in_specs=[hbm] * 7,
         out_specs=vmem,
         scratch_shapes=[
@@ -437,7 +478,8 @@
             pltpu.VMEM((2, WIDTH, CHAN), BF16),
             pltpu.VMEM((HEIGHT, WIDTH, DIM), F32),
             pltpu.VMEM((2, HEIGHT, CHAN), BF16),
-            pltpu.VMEM((2, 2, 16, CHAN), BF16),
+            pltpu.VMEM((2, 2, 16, 128), BF16),
+            pltpu.VMEM((2, 2, 16, 128), BF16),
             pltpu.VMEM((2, HEIGHT, CHAN), BF16),
             pltpu.VMEM((4, BLOCK, 2 * DIM), BF16),
             pltpu.VMEM((4, 2, 8, 128), F32),
@@ -456,9 +498,10 @@
             pltpu.VMEM((2, 2, 2, 1, 128), F32),
             pltpu.VMEM((2, 2, 2, 1, 128), F32),
             pltpu.VMEM((CHIPS, 2, 1, 128), F32),
+            pltpu.VMEM((2, 1, 128), F32),
             pltpu.VMEM((128, 128), F32),
             dma((7,)), dma((8,)), dma((8,)), dma((3, PIECES + 1)), dma((3, PIECES + 1)), dma((2,)), dma((2,)),
-            dma((2,)), dma, dma, dma, dma, dma, dma, pltpu.SemaphoreType.REGULAR((2,)),
+            dma((2,)), dma, dma, dma, dma, dma, dma, dma, dma, pltpu.SemaphoreType.REGULAR((2,)),
         ],
         compiler_params=pltpu.CompilerParams(
             collective_id=0, has_side_effects=True, vmem_limit_bytes=56 * 2**20

time: 51.1 us -> 47.1 us (0.922)
  Pallas kernels: 47.6 us -> 44.9 us
  other arithmetic: 1.79 us -> 0.83 us
    pallas_call x1, Pallas kernels: 47.6 us -> 44.9 us  [shards(): pl.pallas_call(kernel, out_shape=pltpu.VMEM((GROUP, 16, DIM), BF16), in_s...]
    reshape x1, other arithmetic: 1.79 us -> 0.83 us  [shards(): fisher[:, 8 * k:8 * k + 8].astype(F32).reshape(BLOCK, DIM)]
where the time goes in v3:
time: 47.1 us; the launch traced here: 47 us
  Pallas kernels  44.9 us (95%)
  between operations  1.29 us (3%)
  other arithmetic  0.83 us (2%)
    pallas_call x1, Pallas kernels, shards(): pl.pallas_call(kernel, out_shape=pltpu.VMEM((GROUP, 16, DIM), BF16), in_s...  44.9 us

profile of v3, /device:TPU:0, one launch (start us, length us, event | category | flops | bytes accessed | tf_op | source)
XLA Modules:
  0.0 47.0 jit_solution(1157851260196812070)
XLA Ops:
  1.3 44.9 %shard_map.86 = bf16[32,16,256]{2,1,0:T(8,128)(2,1)S(1)} custom-call(bf16[32,64,512]{2,1,0:T(8,128)(2,1)} %features.1, bf16[3,3,512,256]{3,2,1,0:T(8,128)(2,1)} %conv_weight.1, f32[1,256]{1,0:T(1,128)} %bitcast.9, f32[256,256]{1,0:T(8,128)} %means_in.1, f32[256,256]{1,0:T(8,128)} %precisions_in.1, f32[8,1,128]{2,1,0:T(1,128)} %bitcast.8, ...), custom_call_target="tpu_custom_call" | custom-call | tf_op jit(solution)/shard_map/pallas_call | solution.py:465
  46.1 0.8 %bitcast_convert_fusion = (f32[256,256]{1,0:T(8,128)}, f32[256,256]{1,0:T(8,128)}) fusion(bf16[32,16,256]{2,1,0:T(8,128)(2,1)S(1)} %shard_map.86), kind=kLoop, calls=%fused_computation | loop fusion | flops 131072 | bytes 786432 | tf_op jit(solution)/shard_map/reshape | solution.py:514

commit v4 on v3

--- a/solution.py
+++ b/solution.py
@@ -78,7 +78,7 @@
             (bias_in, bias), (count_in, count), (conv_weight, w),
         ))
     ]
-    for load in loads:
+    for load in loads[:6]:
         load.start()
 
     barrier = pltpu.get_barrier_semaphore()
@@ -130,11 +130,9 @@
     offsets_across, offsets_partner, offsets_onward = (
         offset_copy(comp, 0, across), offset_copy(comp, 1, partner), offset_copy(far, 2, partner)
     )
-    for copy in to_across + to_partner:
-        copy.start()
-    hear(x_peers, 0)
 
     loads[2].wait()
+    loads[6].start()
     halos = []
 
     def halo(index, down, right, src, dst):
@@ -165,6 +163,10 @@
         )
         corners_out[side, end] = spread.astype(BF16)
         halo(index, down, right, corners_out.at[side, end], corners.at[side, end])
+
+    for copy in to_across + to_partner:
+        copy.start()
+    hear(x_peers, 0)
 
     loads[3].wait()
     lines = logits[...]
@@ -311,6 +313,7 @@
         copy.wait()
     spread_offsets(far)
     spread_offsets(beyond)
+    pl.semaphore_wait(heard.at[1], 3)
     limit = count[...]
     for i in range(PATCHES // CHUNK):
         at = slice(i * CHUNK, (i + 1) * CHUNK)
@@ -333,8 +336,6 @@
             else:
                 zeroth[rows] += part
 
-    pl.semaphore_wait(heard.at[1], 3)
-
     tally = jnp.broadcast_to(limit.astype(F32), (1, 128))
     for h, order in ((0, 0), (1, 2)):
         for half in range(2):
@@ -343,7 +344,6 @@
                 ref[h, half, 0] = jnp.sum(zeroth[start : start + 128].T, axis=0, keepdims=True)
                 ref[h, half, 1] = tally
     sums_copy = remote(sums_give, sums_take, sums_pair.at[0], sums_pair.at[1], partner)
-    sums_copy.start()
 
     def statistics(place):
         stats = jnp.dot(gamma[place * BLOCK : (place + 1) * BLOCK, :], design[...], preferred_element_type=F32)
@@ -353,21 +353,35 @@
 
     pair = []
     for k in range(2):
+        pair.append(remote(give.at[k], take.at[k], pair_send.at[k], pair_recv.at[k], partner))
+    for k in (1, 0):
         give[k] = statistics(2 * k + 1).astype(BF16)
-        pair.append(remote(give.at[k], take.at[k], pair_send.at[k], pair_recv.at[k], partner))
         pair[k].start()
+        if k == 1:
+            sums_copy.start()
 
     sums_copy.wait()
     sums_held[...] += sums_take[...]
 
+    def apart(number):
+        return [number, number + 1 - 2 * lax.rem(number, 2), lax.rem(number + 2, 4), 3 - number]
+
+    x_apart, z_apart = apart(row // 2), apart(col)
+    y_apart = [lower, 1 - lower]
+
+    def owners(k):
+        hops = [0, 1, 2, 1]
+        places = [(dx, dy, dz) for dx in range(4) for dy in range(2) for dz in range(4)]
+        places = [p for p in places if k or any(p)]
+        return sorted(places, key=lambda p: -(hops[p[0]] + hops[p[1] + 2 * k] + hops[p[2]]))
+
     def scatter(k):
-        def send(step, carry):
-            step = 2 * step + k
-            to = lax.rem(me + step, CHIPS)
-            remote(held.at[k, to // 2], landed.at[CHIPS - step], scatter_send, scatter_recv, chip(to)).start()
-            return carry
-
-        lax.fori_loop(1 - k, GROUP, send, 0)
+        for dx, dy, dz in owners(k):
+            to_row, to_col = 2 * x_apart[dx] + y_apart[dy], z_apart[dz]
+            remote(
+                held.at[k, to_row * 4 + to_col], landed.at[k * GROUP + dx * 8 + dy * 4 + dz],
+                scatter_send, scatter_recv, (to_row, to_col, far if k else comp),
+            ).start()
 
     owner = row * 4 + col
     adds = lax.rem(owner, 16) == 5
@@ -383,7 +397,7 @@
             def _():
                 lines_out[-1][1].start()
 
-    for k in range(2):
+    for k in (1, 0):
         mine = statistics(2 * k)
         pair[k].wait()
         held[k] = (mine + take[k].astype(F32)).astype(BF16)
@@ -444,14 +458,11 @@
     ) / jnp.sqrt(2.0 * patches * share)
     gathered[owner] = jnp.concatenate([mean_fisher, var_fisher], axis=0).astype(BF16)
 
-    def gather(step, carry):
-        to = lax.rem(owner + step, GROUP)
+    for dx, dy, dz in owners(0):
         remote(
-            gathered.at[owner], gathered.at[owner], gather_send, gather_recv, (to // 4, lax.rem(to, 4), comp)
+            gathered.at[owner], gathered.at[owner], gather_send, gather_recv,
+            (2 * x_apart[dx] + y_apart[dy], z_apart[dz], comp),
         ).start()
-        return carry
-
-    lax.fori_loop(1, GROUP, gather, 0)
     others = remote(gathered.at[pl.ds(1, GROUP - 1)], gathered.at[pl.ds(1, GROUP - 1)], gather_send, gather_recv, partner)
     others.wait_send()
     others.wait_recv()

time: 47.1 us -> 42.2 us (0.90)
  Pallas kernels: 44.9 us -> 39.9 us
    pallas_call x1, Pallas kernels: 44.9 us -> 39.9 us  [shards(): pl.pallas_call(kernel, out_shape=pltpu.VMEM((GROUP, 16, DIM), BF16), in_s...]
where the time goes in v4:
time: 42.2 us; the launch traced here: 42 us
  Pallas kernels  39.9 us (95%)
  between operations  1.29 us (3%)
  other arithmetic  0.83 us (2%)
    pallas_call x1, Pallas kernels, shards(): pl.pallas_call(kernel, out_shape=pltpu.VMEM((GROUP, 16, DIM), BF16), in_s...  39.9 us

profile of v4, /device:TPU:0, one launch (start us, length us, event | category | flops | bytes accessed | tf_op | source)
XLA Modules:
  0.0 42.0 jit_solution(7253965067419816579)
XLA Ops:
  1.3 39.9 %shard_map.86 = bf16[32,16,256]{2,1,0:T(8,128)(2,1)S(1)} custom-call(bf16[32,64,512]{2,1,0:T(8,128)(2,1)} %features.1, bf16[3,3,512,256]{3,2,1,0:T(8,128)(2,1)} %conv_weight.1, f32[1,256]{1,0:T(1,128)} %bitcast.9, f32[256,256]{1,0:T(8,128)} %means_in.1, f32[256,256]{1,0:T(8,128)} %precisions_in.1, f32[8,1,128]{2,1,0:T(1,128)} %bitcast.8, ...), custom_call_target="tpu_custom_call" | custom-call | tf_op jit(solution)/shard_map/pallas_call | solution.py:476
  41.2 0.8 %bitcast_convert_fusion = (f32[256,256]{1,0:T(8,128)}, f32[256,256]{1,0:T(8,128)}) fusion(bf16[32,16,256]{2,1,0:T(8,128)(2,1)S(1)} %shard_map.86), kind=kLoop, calls=%fused_computation | loop fusion | flops 131072 | bytes 786432 | tf_op jit(solution)/shard_map/reshape | solution.py:525

commit v5 on v4

--- a/solution.py
+++ b/solution.py
@@ -301,14 +301,12 @@
         peak, grown, total = score(i, comp, comp + 1 - 2 * core)
         mass[:, i * CHUNK : (i + 1) * CHUNK] = grown
         near.append((peak, total))
-        if i >= 1:
-            to_across[i - 1].wait()
-            onward[i - 1].start()
 
     offsets_across.wait()
     offsets_onward.start()
-    to_across[PIECES - 1].wait()
-    onward[PIECES - 1].start()
+    for piece in range(PIECES):
+        to_across[piece].wait()
+        onward[piece].start()
     for copy in [offsets_onward] + onward:
         copy.wait()
     spread_offsets(far)

time: 42.2 us -> 41.7 us (0.988)
  Pallas kernels: 39.9 us -> 39.4 us
    pallas_call x1, Pallas kernels: 39.9 us -> 39.4 us  [shards(): pl.pallas_call(kernel, out_shape=pltpu.VMEM((GROUP, 16, DIM), BF16), in_s...]
where the time goes in v5:
time: 41.7 us; the launch traced here: 41.5 us
  Pallas kernels  39.4 us (94%)
  between operations  1.29 us (3%)
  other arithmetic  0.83 us (2%)
    pallas_call x1, Pallas kernels, shards(): pl.pallas_call(kernel, out_shape=pltpu.VMEM((GROUP, 16, DIM), BF16), in_s...  39.4 us

profile of v5, /device:TPU:0, one launch (start us, length us, event | category | flops | bytes accessed | tf_op | source)
XLA Modules:
  0.0 41.5 jit_solution(8900584878096110666)
XLA Ops:
  1.3 39.4 %shard_map.86 = bf16[32,16,256]{2,1,0:T(8,128)(2,1)S(1)} custom-call(bf16[32,64,512]{2,1,0:T(8,128)(2,1)} %features.1, bf16[3,3,512,256]{3,2,1,0:T(8,128)(2,1)} %conv_weight.1, f32[1,256]{1,0:T(1,128)} %bitcast.9, f32[256,256]{1,0:T(8,128)} %means_in.1, f32[256,256]{1,0:T(8,128)} %precisions_in.1, f32[8,1,128]{2,1,0:T(1,128)} %bitcast.8, ...), custom_call_target="tpu_custom_call" | custom-call | tf_op jit(solution)/shard_map/pallas_call | solution.py:474
  40.7 0.8 %bitcast_convert_fusion = (f32[256,256]{1,0:T(8,128)}, f32[256,256]{1,0:T(8,128)}) fusion(bf16[32,16,256]{2,1,0:T(8,128)(2,1)S(1)} %shard_map.86), kind=kLoop, calls=%fused_computation | loop fusion | flops 131072 | bytes 786432 | tf_op jit(solution)/shard_map/reshape | solution.py:523
